TPU v7x, 32 devices: a whole 2x2x4 slice. The times are simulated.
32 devices in a mesh: diag: 16 (over z, y, core), tri: 2 (over x).
Axes of the slice: x: 2, y: 2, z: 4, core: 2. Of those that a mesh axis runs over, the one named last changes fastest.
Arguments:
- trial_sets: bfloat16 [2, 12, 65536], P(None, None, 'diag'), may hold values from -6 to 6
- tile_values: bfloat16 [16, 2, 192, 128, 128], P('diag', 'tri'), may hold values from -0.109375 to 0.109375
- tile_pattern: int32 [16, 2, 2, 192], P('diag', 'tri'), may hold values from 0 to 31, as said below
- tile_count: int32 [16, 2], P('diag', 'tri'), may hold values from 48 to 192, as said below
Outputs:
- images: float32 [2, 12, 65536], P(None, None, ('diag', 'tri'))
Inputs may be any that keep to these rules, and one draw needn't show every extreme that they name: `tile_pattern`: within each stored block the live and padding slots name distinct tiles. `tile_count`: some stored block has all 192 slots live.
All inputs are finite; a program needn't handle non-finite values.
Results may differ from a plain program's by a relative error of at most 0.0003.
Values may be sent and summed in bfloat16 or wider, within the bound.
No kernel may reach another device: no remote copies, remote signals or barrier semaphores. Data moves between devices by JAX's collectives and lax.ppermute only.
A program may use at most 64 MiB of HBM per device.

v0:
```python
import functools
import math

import jax
import jax.numpy as jnp
from jax import lax
from jax.experimental import pallas as pl
from jax.experimental.pallas import tpu as pltpu
from jax.sharding import PartitionSpec as P

F32 = jnp.float32
VMEM_BYTES = 16 << 20
WIDE_BYTES = 24 << 20
ROWS = 8
ORDER = 13
AHEAD = 3


def fill_vectors(vectors_ref, packed_ref, tile):
    blocks, padded, _ = packed_ref.shape
    vecs, sets, _ = vectors_ref.shape
    for b in range(blocks):
        slab = vectors_ref[:, :, b * tile : (b + 1) * tile].reshape(vecs * sets, tile)
        packed_ref[b] = jnp.concatenate(
            [slab, jnp.zeros((padded - vecs * sets, tile), slab.dtype)], axis=0
        )


def add_products(start, size, count, pattern_ref, source, target, packed_ref, tiles_ref, sums_ref):
    blocks, columns, tile = sums_ref.shape
    padded = packed_ref.shape[1]
    results = []
    for s in range(start, start + size, 2):
        left = jnp.concatenate([packed_ref[pattern_ref[source, s + e]] for e in range(2)], axis=0)
        right = jnp.concatenate([tiles_ref[s + e] for e in range(2)], axis=1)
        both = jnp.dot(left, right, preferred_element_type=F32)
        places = [jnp.where(s + e < count, pattern_ref[target, s + e], blocks - 1) for e in range(2)]
        parts = [both[e * padded : e * padded + columns, e * tile : (e + 1) * tile] for e in range(2)]
        results.append((places, parts))
    for (place, other), (part, last) in results:
        held, total = sums_ref[place], sums_ref[other]
        sums_ref[place] = held + part
        sums_ref[other] = total + (last + jnp.where(place == other, part, 0.0))


def write_message(message_ref, part):
    tile = part.shape[-1]
    flat = part.reshape(-1, ROWS, tile)
    top = jnp.max(jnp.abs(flat), axis=0)
    power = ORDER - jnp.floor(jnp.log2(jnp.maximum(top, 2.0**-100)))
    groups = flat.shape[0]
    message_ref[:groups] = flat * jnp.exp2(power)[None]
    message_ref[groups] = power


def read_message(message_ref, shape):
    groups = message_ref.shape[0] - 1
    return (message_ref[:groups] * jnp.exp2(-message_ref[groups])[None]).reshape(shape)


def first_kernel(steps, count_ref, pattern_hbm, vectors_hbm, tiles_hbm, *rest):
    turned_ref, *messages = rest[:-7]
    pattern_ref, vectors_ref, packed_ref, sums_ref, tiles_ref, small_sem, tile_sem = rest[-7:]
    parts = len(messages)
    blocks = packed_ref.shape[0]
    held = blocks // parts
    tri_index = lax.axis_index("tri")
    loads = [
        pltpu.make_async_copy(vectors_hbm, vectors_ref, small_sem.at[0]),
        pltpu.make_async_copy(pattern_hbm.at[0, 0], pattern_ref, small_sem.at[1]),
    ]
    streams = [
        pltpu.make_async_copy(
            tiles_hbm.at[0, 0, pl.ds(start, size)], tiles_ref.at[pl.ds(start, size)], tile_sem.at[k]
        )
        for k, (start, size) in enumerate(steps)
    ]
    for copy in loads + streams[:AHEAD]:
        copy.start()
    sums_ref[...] = jnp.zeros_like(sums_ref)
    for copy in loads:
        copy.wait()
    fill_vectors(vectors_ref, packed_ref, tiles_ref.shape[1])
    count = count_ref[0, 0]
    for k, (start, size) in enumerate(steps):
        streams[k].wait()
        if k + AHEAD < len(steps):
            streams[k + AHEAD].start()

        @pl.when(count > start)
        def _():
            add_products(
                start, size, count, pattern_ref, 0, 1, packed_ref, tiles_ref, sums_ref
            )
            for s in range(start, start + size):
                turned_ref[s] = tiles_ref[s].T

    for d, message_ref in enumerate(messages, 1):
        part = lax.rem(tri_index + d, parts)
        write_message(message_ref, sums_ref[pl.ds(part * held, held)])


def second_kernel(steps, count_ref, pattern_ref, vectors_ref, passed_ref, turned_ref, *rest):
    parts = (len(rest) - 2) // 3
    own, (keep_ref, *messages), (packed_ref, sums_ref) = rest[:parts], rest[parts:-2], rest[-2:]
    messages, later = messages[: parts - 1], messages[parts - 1 :]
    blocks = packed_ref.shape[0]
    held = blocks // parts
    tri_index = lax.axis_index("tri")

    @pl.when(tri_index == 0)
    def _():
        for d, own_ref in enumerate(own, 1):
            d %= parts
            sums_ref[d * held : (d + 1) * held] = read_message(own_ref, keep_ref.shape)
        fill_vectors(vectors_ref, packed_ref, turned_ref.shape[1])

    @pl.when(tri_index != 0)
    def _():
        sums_ref[...] = jnp.zeros_like(sums_ref)
        fill_vectors(passed_ref, packed_ref, turned_ref.shape[1])

    count = count_ref[0, 0]
    for start, size in steps:

        @pl.when(count > start)
        def _():
            add_products(
                start, size, count, pattern_ref, 1, 0, packed_ref, turned_ref, sums_ref
            )

    keep_ref[...] = sums_ref[pl.ds(tri_index * held, held)]
    for d, message_ref in enumerate(messages, 1):
        part = lax.rem(tri_index + d, parts)
        write_message(message_ref, sums_ref[pl.ds(part * held, held)])
    for own_ref, later_ref in zip(own, later):
        later_ref[...] = own_ref[...]

    @pl.when(tri_index == 0)
    def _():
        for message_ref, later_ref in zip(messages, later):
            later_ref[...] = message_ref[...]


def add_kernel(skipped, kept_ref, *rest):
    *messages, total_ref = rest
    tri_index = lax.axis_index("tri")
    total_ref[...] = kept_ref[...]
    for skip, message_ref in zip(skipped, messages):

        @pl.when(tri_index != skip)
        def _(message_ref=message_ref):
            total_ref[...] += read_message(message_ref, kept_ref.shape)


def last_kernel(kept_ref, message_ref, out_ref, total_ref):
    blocks, _, tile = kept_ref.shape
    total_ref[...] = kept_ref[...]

    @pl.when(lax.axis_index("tri") != 0)
    def _():
        total_ref[...] += read_message(message_ref, kept_ref.shape)

    vecs, sets, _ = out_ref.shape
    for b in range(blocks):
        out_ref[:, :, b * tile : (b + 1) * tile] = total_ref[b].reshape(vecs, sets, tile)


def local(trial_sets, tile_values, tile_pattern, tile_count):
    set_count, vec_count, row_total = trial_sets.shape
    columns = set_count * vec_count
    tile_total, tile = tile_values.shape[2:4]
    blocks = row_total // tile
    unit = math.gcd(tile_total, 48)
    steps = [(k * unit, unit) for k in range(tile_total // unit)]
    half = tile_total // 2
    halves = [(0, half), (half, half)]
    parts = lax.axis_size("tri")
    ring = lax.axis_size("diag")
    held = blocks // parts
    padded = -(-columns // 16) * 16
    message = pltpu.VMEM((held * columns // ROWS + 1, ROWS, tile), F32)
    smem, vmem, hbm = (pl.BlockSpec(memory_space=m) for m in (pltpu.SMEM, pltpu.VMEM, pltpu.HBM))
    scratch = [
        pltpu.VMEM((blocks, padded, tile), jnp.bfloat16),
        pltpu.VMEM((blocks + 1, columns, tile), F32),
    ]
    params = pltpu.CompilerParams(vmem_limit_bytes=VMEM_BYTES)

    def moved(x, way, turn, swap=lambda i: i):
        pairs = [
            (i * parts + t, ((i + way * t) % ring if t else swap(i)) * parts + (t + turn) % parts)
            for i in range(ring)
            for t in range(parts)
        ]
        return lax.ppermute(x, ("diag", "tri"), pairs)

    def beside(i):
        return i ^ 1 if ring % 2 == 0 else (i + 1) % ring

    def aside(i):
        step = ring // 4
        return {0: 1, 1: step + 1, step + 1: step, step: 0}.get(i, i) if step > 1 else i

    def sent(x, *route):
        return moved(x.astype(jnp.float16), *route).astype(F32)

    vectors = trial_sets.transpose(1, 0, 2)
    passed = moved(vectors, 1, 0, beside)
    pattern = tile_pattern.reshape(2, tile_total)
    turned, *own = pl.pallas_call(
        functools.partial(first_kernel, steps),
        out_shape=[pltpu.VMEM((tile_total, tile, tile), tile_values.dtype)] + [message] * parts,
        in_specs=[smem] + [hbm] * 3,
        out_specs=[vmem] * (parts + 1),
        scratch_shapes=[
            pltpu.SMEM((2, tile_total), jnp.int32),
            pltpu.VMEM((vec_count, set_count, row_total), jnp.bfloat16),
            *scratch,
            pltpu.VMEM((tile_total, tile, tile), tile_values.dtype),
            pltpu.SemaphoreType.DMA((2,)),
            pltpu.SemaphoreType.DMA((len(steps),)),
        ],
        compiler_params=pltpu.CompilerParams(vmem_limit_bytes=WIDE_BYTES),
        name="transposed_products",
    )(tile_count, *(pltpu.with_memory_space_constraint(x, pltpu.HBM) for x in (tile_pattern, vectors, tile_values)))
    keep, *rest = pl.pallas_call(
        functools.partial(second_kernel, halves),
        out_shape=[pltpu.VMEM((held, columns, tile), F32)] + [message] * (2 * parts - 1),
        in_specs=[smem] * 2 + [vmem] * (3 + parts),
        out_specs=[vmem] * (2 * parts),
        scratch_shapes=scratch,
        compiler_params=params,
        name="plain_products",
    )(tile_count, pattern, vectors, passed, turned, *own)
    across = [sent(m, 0, d, aside) for d, m in enumerate(rest[: parts - 1], 1)]
    back = [sent(m, -1, d) for d, m in enumerate(rest[parts - 1 : -1], 1)]
    back.append(sent(rest[-1], -1, 0, beside))

    def added(skipped, kept, messages):
        return pl.pallas_call(
            functools.partial(add_kernel, skipped),
            out_shape=pltpu.VMEM((held, columns, tile), F32),
            in_specs=[vmem] * (len(messages) + 1),
            out_specs=vmem,
            compiler_params=params,
            name="sum_of_messages",
        )(kept, *messages)

    kept = added([d % parts for d in range(1, parts)], keep, across)
    kept = added([-1] * (parts - 1), kept, back[:-1])
    images = pl.pallas_call(
        last_kernel,
        out_shape=jax.ShapeDtypeStruct((vec_count, set_count, row_total // parts), F32),
        in_specs=[vmem] * 2,
        out_specs=vmem,
        scratch_shapes=[pltpu.VMEM((held, columns, tile), F32)],
        compiler_params=params,
        name="last_sum",
    )(kept, back[-1])
    return images.transpose(1, 0, 2)


def solution(mesh):
    return jax.shard_map(
        local,
        mesh=mesh,
        in_specs=(
            P(None, None, "diag"),
            P("diag", "tri", None, None, None),
            P("diag", "tri", None, None),
            P("diag", "tri"),
        ),
        out_specs=P(None, None, ("diag", "tri")),
        check_vma=False,
    )
```

profile of v0, /device:TPU:0, one launch (start us, length us, event | category | flops | bytes accessed | tf_op | source)
XLA Modules:
  0.0 18.2 jit_solution(1291083683964417860)
XLA Ops:
  0.0 0.0 copy-start
  0.0 0.0 copy-start.1
  0.0 0.5 %collective-permute-start = (bf16[12,2,4096]{2,1,0:T(2,128)(2,1)}, bf16[12,2,4096]{2,1,0:T(2,128)(2,1)S(1)}, u32[]{:S(2)}, u32[]{:S(2)}) collective-permute-start(bf16[12,2,4096]{2,1,0:T(2,128)(2,1)} %bitcast.3), channel_id=1, source_target_pairs={{0,2},{1,3},{2,0},{3,5},{4,6},{5,7},{6,4},{7,9},{8,10},{9,11},{10,... | collective-permute-start | bytes 589832 | tf_op jit(solution)/shard_map/ppermute | solution.py:196
  1.1 4.0 %transposed_products.1 = (bf16[192,128,128]{2,1,0:T(8,128)(2,1)S(1)}, f32[49,8,128]{2,1,0:T(8,128)S(1)}, f32[49,8,128]{2,1,0:T(8,128)S(1)}) custom-call(s32[1,1]{1,0:T(1,128)S(6)} %copy.5.count_ref, s32[1,1,2,192]{3,2,1,0:T(2,128)} %pattern_hbm.1, bf16[12,2,4096]{2,1,0:T(2,128)(2,1)} %bitcast.4, bf16[1,1,192,128,128]{4,3,2,1,0:T(8,128)(2,1)} %tiles_hbm.1), custom_call_target="tpu_custom_call" | custom-call | tf_op jit(solution)/shard_map/transposed_products/pallas_call | solution.py:211
  5.1 0.0 collective-permute-done.passed_ref
  5.1 0.0 copy-done
  5.1 0.0 copy-done.1
  5.1 2.1 %plain_products.1 = (f32[16,24,128]{2,1,0:T(8,128)S(1)}, f32[49,8,128]{2,1,0:T(8,128)S(1)}, f32[49,8,128]{2,1,0:T(8,128)S(1)}, f32[49,8,128]{2,1,0:T(8,128)S(1)}) custom-call(s32[1,1]{1,0:T(1,128)S(6)} %copy.5.count_ref, s32[2,192]{1,0:T(2,128)S(1)} %bitcast.6, bf16[12,2,4096]{2,1,0:T(2,128)(2,1)S(1)} %bitcast.5, ...), custom_call_target="tpu_custom_call" | custom-call | tf_op jit(solution)/shard_map/plain_products/pallas_call | solution.py:227
  7.3 3.8 %collective-permute-start.1 = (f16[49,8,128]{2,1,0:T(8,128)(2,1)S(1)}, f16[49,8,128]{2,1,0:T(8,128)(2,1)S(1)}, u32[]{:S(2)}, u32[]{:S(2)}) collective-permute-start(f16[49,8,128]{2,1,0:T(8,128)(2,1)S(1)} %convert_element_type.18), channel_id=1, source_target_pairs={{0,3},{1,0},{2,11},{3,2},{4,5},{5,4},{6,7},{7,6},{8,1},{9,8},{10,9... | collective-permute-start | bytes 301064 | tf_op jit(solution)/shard_map/ppermute | solution.py:196
  11.1 1.6 %collective-permute-start.2 = (f16[49,8,128]{2,1,0:T(8,128)(2,1)S(1)}, f16[49,8,128]{2,1,0:T(8,128)(2,1)S(1)}, u32[]{:S(2)}, u32[]{:S(2)}) collective-permute-start(f16[49,8,128]{2,1,0:T(8,128)(2,1)S(1)} %convert_element_type.20), channel_id=1, source_target_pairs={{0,1},{1,30},{2,3},{3,0},{4,5},{5,2},{6,7},{7,4},{8,9},{9,6},{10,1... | collective-permute-start | bytes 301064 | tf_op jit(solution)/shard_map/ppermute | solution.py:196
  12.7 0.1 collective-permute-start.3
  12.7 4.5 %collective-permute-done.1 = f16[49,8,128]{2,1,0:T(8,128)(2,1)S(1)} collective-permute-done((f16[49,8,128]{2,1,0:T(8,128)(2,1)S(1)}, f16[49,8,128]{2,1,0:T(8,128)(2,1)S(1)}, u32[]{:S(2)}, u32[]{:S(2)}) %collective-permute-start.1) | collective-permute-done | bytes 100384 | tf_op jit(solution)/shard_map/ppermute | solution.py:196
  17.3 0.0 collective-permute-done.2
  17.4 0.0 collective-permute-done.3
  17.4 0.8 %last_sum.1 = f32[12,2,2048]{2,1,0:T(2,128)} custom-call(f32[16,24,128]{2,1,0:T(8,128)S(1)} %sum_of_messages.3.kept_ref, f32[49,8,128]{2,1,0:T(8,128)S(1)} %convert_element_type.23.message_ref), custom_call_target="tpu_custom_call" | custom-call | tf_op jit(solution)/shard_map/last_sum/pallas_call | solution.py:252
  (8 shorter events, 0.2 us)
Async XLA Ops:
  0.0 5.1 %copy-start = (bf16[2,12,4096]{2,0,1:T(2,128)(2,1)S(1)}, bf16[2,12,4096]{2,0,1:T(2,128)(2,1)}, u32[]{:S(2)}) copy-start(bf16[2,12,4096]{2,0,1:T(2,128)(2,1)} %param.4) | copy-start | bytes 589828
  0.0 5.1 %copy-start.1 = (s32[1,1,2,192]{3,2,1,0:T(2,128)S(1)}, s32[1,1,2,192]{3,2,1,0:T(2,128)}, u32[]{:S(2)}) copy-start(s32[1,1,2,192]{3,2,1,0:T(2,128)} %pattern_hbm.1) | copy-start | bytes 4612
  0.0 5.1 %collective-permute-start = (bf16[12,2,4096]{2,1,0:T(2,128)(2,1)}, bf16[12,2,4096]{2,1,0:T(2,128)(2,1)S(1)}, u32[]{:S(2)}, u32[]{:S(2)}) collective-permute-start(bf16[12,2,4096]{2,1,0:T(2,128)(2,1)} %bitcast.3), channel_id=1, source_target_pairs={{0,2},{1,3},{2,0},{3,5},{4,6},{5,7},{6,4},{7,9},{8,10},{9,11},{10,... | collective-permute-start | bytes 589832 | tf_op jit(solution)/shard_map/ppermute | solution.py:196
  7.3 10.0 %collective-permute-start.1 = (f16[49,8,128]{2,1,0:T(8,128)(2,1)S(1)}, f16[49,8,128]{2,1,0:T(8,128)(2,1)S(1)}, u32[]{:S(2)}, u32[]{:S(2)}) collective-permute-start(f16[49,8,128]{2,1,0:T(8,128)(2,1)S(1)} %convert_element_type.18), channel_id=1, source_target_pairs={{0,3},{1,0},{2,11},{3,2},{4,5},{5,4},{6,7},{7,6},{8,1},{9,8},{10,9... | collective-permute-start | bytes 301064 | tf_op jit(solution)/shard_map/ppermute | solution.py:196
  11.1 6.2 %collective-permute-start.2 = (f16[49,8,128]{2,1,0:T(8,128)(2,1)S(1)}, f16[49,8,128]{2,1,0:T(8,128)(2,1)S(1)}, u32[]{:S(2)}, u32[]{:S(2)}) collective-permute-start(f16[49,8,128]{2,1,0:T(8,128)(2,1)S(1)} %convert_element_type.20), channel_id=1, source_target_pairs={{0,1},{1,30},{2,3},{3,0},{4,5},{5,2},{6,7},{7,4},{8,9},{9,6},{10,1... | collective-permute-start | bytes 301064 | tf_op jit(solution)/shard_map/ppermute | solution.py:196
  12.7 4.7 %collective-permute-start.3 = (f16[49,8,128]{2,1,0:T(8,128)(2,1)S(1)}, f16[49,8,128]{2,1,0:T(8,128)(2,1)S(1)}, u32[]{:S(2)}, u32[]{:S(2)}) collective-permute-start(f16[49,8,128]{2,1,0:T(8,128)(2,1)S(1)} %convert_element_type.22), channel_id=1, source_target_pairs={{0,2},{1,31},{2,0},{3,1},{4,6},{5,3},{6,4},{7,5},{8,10},{9,7},{10,... | collective-permute-start | bytes 301064 | tf_op jit(solution)/shard_map/ppermute | solution.py:196
where the time goes:
time: 18.2 us
  Pallas kernels  6.94 us (38%)
  starting transfers between devices  5.84 us (32%)
  waiting for transfers between devices  4.54 us (25%)
  between operations  0.76 us (4%)
    ppermute x4, starting transfers between devices, moved(): return lax.ppermute(x, ('diag', 'tri'), pairs)  5.84 us
    ppermute x4, waiting for transfers between devices, moved(): return lax.ppermute(x, ('diag', 'tri'), pairs)  4.54 us
    pallas_call x1, Pallas kernels, local(): pl.pallas_call(functools.partial(first_kernel, steps), out_shape=[pltpu.V...  3.96 us
    pallas_call x1, Pallas kernels, local(): pl.pallas_call(functools.partial(second_kernel, halves), out_shape=[pltpu...  2.15 us
    pallas_call x1, Pallas kernels, local(): pl.pallas_call(last_kernel, out_shape=jax.ShapeDtypeStruct((vec_count, se...  0.75 us
  transfers between devices with their start and end apart: 4, of which 1 were waited for; matrix products, arithmetic and copies ran while one was open for 0% of the time, Pallas kernels for 22%

commit v1 on v0

--- a/solution.py
+++ b/solution.py
@@ -121,20 +121,18 @@
         fill_vectors(passed_ref, packed_ref, turned_ref.shape[1])
 
     count = count_ref[0, 0]
-    for start, size in steps:
-
-        @pl.when(count > start)
+    for fewest, size in steps:
+
+        @pl.when((count > fewest) & (count <= size))
         def _():
             add_products(
-                start, size, count, pattern_ref, 1, 0, packed_ref, turned_ref, sums_ref
+                0, size, count, pattern_ref, 1, 0, packed_ref, turned_ref, sums_ref
             )
 
     keep_ref[...] = sums_ref[pl.ds(tri_index * held, held)]
     for d, message_ref in enumerate(messages, 1):
         part = lax.rem(tri_index + d, parts)
         write_message(message_ref, sums_ref[pl.ds(part * held, held)])
-    for own_ref, later_ref in zip(own, later):
-        later_ref[...] = own_ref[...]
 
     @pl.when(tri_index == 0)
     def _():
@@ -174,7 +172,7 @@
     unit = math.gcd(tile_total, 48)
     steps = [(k * unit, unit) for k in range(tile_total // unit)]
     half = tile_total // 2
-    halves = [(0, half), (half, half)]
+    halves = [(0, half), (half, tile_total)]
     parts = lax.axis_size("tri")
     ring = lax.axis_size("diag")
     held = blocks // parts
@@ -230,6 +228,7 @@
         in_specs=[smem] * 2 + [vmem] * (3 + parts),
         out_specs=[vmem] * (2 * parts),
         scratch_shapes=scratch,
+        input_output_aliases={5 + d: parts + d for d in range(parts)},
         compiler_params=params,
         name="plain_products",
     )(tile_count, pattern, vectors, passed, turned, *own)

time: 18.2 us -> 17.8 us (0.978)
  starting transfers between devices: 5.84 us -> 7.05 us
  waiting for transfers between devices: 4.54 us -> 3.52 us
  Pallas kernels: 6.94 us -> 6.26 us
    ppermute x4, starting transfers between devices: 5.84 us -> 7.05 us  [moved(): return lax.ppermute(x, ('diag', 'tri'), pairs)]
    ppermute x4, waiting for transfers between devices: 4.54 us -> 3.52 us  [moved(): return lax.ppermute(x, ('diag', 'tri'), pairs)]
    pallas_call x1, Pallas kernels: 3.96 us -> 3.36 us  [local(): pl.pallas_call(functools.partial(first_kernel, steps), out_shape=[pltpu.V...]
  transfers between devices with their start and end apart: 4 -> 4, of which waited for: 1 -> 1; matrix products, arithmetic and copies ran while one was open for 0% -> 0% of each run, Pallas kernels for 22% -> 19%
where the time goes in v1:
time: 17.8 us; the launch traced here: 17.7 us
  starting transfers between devices  7.05 us (40%)
  Pallas kernels  6.26 us (35%)
  waiting for transfers between devices  3.52 us (20%)
  between operations  0.76 us (4%)
    ppermute x4, starting transfers between devices, moved(): return lax.ppermute(x, ('diag', 'tri'), pairs)  7.05 us
    ppermute x4, waiting for transfers between devices, moved(): return lax.ppermute(x, ('diag', 'tri'), pairs)  3.52 us
    pallas_call x1, Pallas kernels, local(): pl.pallas_call(functools.partial(first_kernel, steps), out_shape=[pltpu.V...  3.36 us
    pallas_call x1, Pallas kernels, local(): pl.pallas_call(functools.partial(second_kernel, halves), out_shape=[pltpu...  2.07 us
    pallas_call x1, Pallas kernels, local(): pl.pallas_call(last_kernel, out_shape=jax.ShapeDtypeStruct((vec_count, se...  0.75 us
  transfers between devices with their start and end apart: 4, of which 1 were waited for; matrix products, arithmetic and copies ran while one was open for 0% of the time, Pallas kernels for 19%

profile of v1, /device:TPU:0, one launch (start us, length us, event | category | flops | bytes accessed | tf_op | source)
XLA Modules:
  0.0 17.7 jit_solution(5108049701548616190)
XLA Ops:
  0.0 0.0 copy-start
  0.0 0.0 copy-start.1
  0.0 0.5 %collective-permute-start = (bf16[12,2,4096]{2,1,0:T(2,128)(2,1)}, bf16[12,2,4096]{2,1,0:T(2,128)(2,1)S(1)}, u32[]{:S(2)}, u32[]{:S(2)}) collective-permute-start(bf16[12,2,4096]{2,1,0:T(2,128)(2,1)} %bitcast.3), channel_id=1, source_target_pairs={{0,2},{1,3},{2,0},{3,5},{4,6},{5,7},{6,4},{7,9},{8,10},{9,11},{10,... | collective-permute-start | bytes 589832 | tf_op jit(solution)/shard_map/ppermute | solution.py:194
  1.1 3.4 %transposed_products.1 = (bf16[192,128,128]{2,1,0:T(8,128)(2,1)S(1)}, f32[49,8,128]{2,1,0:T(8,128)S(1)}, f32[49,8,128]{2,1,0:T(8,128)S(1)}) custom-call(s32[1,1]{1,0:T(1,128)S(6)} %copy.9.count_ref, s32[1,1,2,192]{3,2,1,0:T(2,128)} %pattern_hbm.1, bf16[12,2,4096]{2,1,0:T(2,128)(2,1)} %bitcast.4, bf16[1,1,192,128,128]{4,3,2,1,0:T(8,128)(2,1)} %tiles_hbm.1), custom_call_target="tpu_custom_call" | custom-call | tf_op jit(solution)/shard_map/transposed_products/pallas_call | solution.py:209
  4.5 0.0 collective-permute-done.passed_ref
  4.5 0.0 copy-done
  4.5 0.0 copy-done.1
  4.5 2.1 %plain_products.1 = (f32[16,24,128]{2,1,0:T(8,128)S(1)}, f32[49,8,128]{2,1,0:T(8,128)S(1)}, f32[49,8,128]{2,1,0:T(8,128)S(1)}, f32[49,8,128]{2,1,0:T(8,128)S(1)}) custom-call(s32[1,1]{1,0:T(1,128)S(6)} %copy.9.count_ref, s32[2,192]{1,0:T(2,128)S(1)} %bitcast.6, bf16[12,2,4096]{2,1,0:T(2,128)(2,1)S(1)} %bitcast.5, ...), custom_call_target="tpu_custom_call", output_to_operand_aliasing={{2}: (5, {}), {3}: (6, {})} | custom-call | tf_op jit(solution)/shard_map/plain_products/pallas_call | solution.py:225
  6.6 3.1 %collective-permute-start.1 = (f16[49,8,128]{2,1,0:T(8,128)(2,1)S(1)}, f16[49,8,128]{2,1,0:T(8,128)(2,1)S(1)}, u32[]{:S(2)}, u32[]{:S(2)}) collective-permute-start(f16[49,8,128]{2,1,0:T(8,128)(2,1)S(1)} %convert_element_type.18), channel_id=1, source_target_pairs={{0,3},{1,0},{2,11},{3,2},{4,5},{5,4},{6,7},{7,6},{8,1},{9,8},{10,9... | collective-permute-start | bytes 301064 | tf_op jit(solution)/shard_map/ppermute | solution.py:194
  9.7 3.4 %collective-permute-start.2 = (f16[49,8,128]{2,1,0:T(8,128)(2,1)S(1)}, f16[49,8,128]{2,1,0:T(8,128)(2,1)S(1)}, u32[]{:S(2)}, u32[]{:S(2)}) collective-permute-start(f16[49,8,128]{2,1,0:T(8,128)(2,1)S(1)} %convert_element_type.20), channel_id=1, source_target_pairs={{0,1},{1,30},{2,3},{3,0},{4,5},{5,2},{6,7},{7,4},{8,9},{9,6},{10,1... | collective-permute-start | bytes 301064 | tf_op jit(solution)/shard_map/ppermute | solution.py:194
  13.2 0.1 collective-permute-start.3
  13.3 3.5 %collective-permute-done.1 = f16[49,8,128]{2,1,0:T(8,128)(2,1)S(1)} collective-permute-done((f16[49,8,128]{2,1,0:T(8,128)(2,1)S(1)}, f16[49,8,128]{2,1,0:T(8,128)(2,1)S(1)}, u32[]{:S(2)}, u32[]{:S(2)}) %collective-permute-start.1) | collective-permute-done | bytes 100384 | tf_op jit(solution)/shard_map/ppermute | solution.py:194
  16.8 0.0 collective-permute-done.2
  16.9 0.0 collective-permute-done.3
  17.0 0.8 %last_sum.1 = f32[12,2,2048]{2,1,0:T(2,128)} custom-call(f32[16,24,128]{2,1,0:T(8,128)S(1)} %sum_of_messages.3.kept_ref, f32[49,8,128]{2,1,0:T(8,128)S(1)} %convert_element_type.23.message_ref), custom_call_target="tpu_custom_call" | custom-call | tf_op jit(solution)/shard_map/last_sum/pallas_call | solution.py:251
  (8 shorter events, 0.2 us)
Async XLA Ops:
  0.0 4.5 %copy-start = (bf16[2,12,4096]{2,0,1:T(2,128)(2,1)S(1)}, bf16[2,12,4096]{2,0,1:T(2,128)(2,1)}, u32[]{:S(2)}) copy-start(bf16[2,12,4096]{2,0,1:T(2,128)(2,1)} %param.4) | copy-start | bytes 589828
  0.0 4.5 %copy-start.1 = (s32[1,1,2,192]{3,2,1,0:T(2,128)S(1)}, s32[1,1,2,192]{3,2,1,0:T(2,128)}, u32[]{:S(2)}) copy-start(s32[1,1,2,192]{3,2,1,0:T(2,128)} %pattern_hbm.1) | copy-start | bytes 4612
  0.0 4.5 %collective-permute-start = (bf16[12,2,4096]{2,1,0:T(2,128)(2,1)}, bf16[12,2,4096]{2,1,0:T(2,128)(2,1)S(1)}, u32[]{:S(2)}, u32[]{:S(2)}) collective-permute-start(bf16[12,2,4096]{2,1,0:T(2,128)(2,1)} %bitcast.3), channel_id=1, source_target_pairs={{0,2},{1,3},{2,0},{3,5},{4,6},{5,7},{6,4},{7,9},{8,10},{9,11},{10,... | collective-permute-start | bytes 589832 | tf_op jit(solution)/shard_map/ppermute | solution.py:194
  6.6 10.2 %collective-permute-start.1 = (f16[49,8,128]{2,1,0:T(8,128)(2,1)S(1)}, f16[49,8,128]{2,1,0:T(8,128)(2,1)S(1)}, u32[]{:S(2)}, u32[]{:S(2)}) collective-permute-start(f16[49,8,128]{2,1,0:T(8,128)(2,1)S(1)} %convert_element_type.18), channel_id=1, source_target_pairs={{0,3},{1,0},{2,11},{3,2},{4,5},{5,4},{6,7},{7,6},{8,1},{9,8},{10,9... | collective-permute-start | bytes 301064 | tf_op jit(solution)/shard_map/ppermute | solution.py:194
  9.7 7.1 %collective-permute-start.2 = (f16[49,8,128]{2,1,0:T(8,128)(2,1)S(1)}, f16[49,8,128]{2,1,0:T(8,128)(2,1)S(1)}, u32[]{:S(2)}, u32[]{:S(2)}) collective-permute-start(f16[49,8,128]{2,1,0:T(8,128)(2,1)S(1)} %convert_element_type.20), channel_id=1, source_target_pairs={{0,1},{1,30},{2,3},{3,0},{4,5},{5,2},{6,7},{7,4},{8,9},{9,6},{10,1... | collective-permute-start | bytes 301064 | tf_op jit(solution)/shard_map/ppermute | solution.py:194
  13.2 3.7 %collective-permute-start.3 = (f16[49,8,128]{2,1,0:T(8,128)(2,1)S(1)}, f16[49,8,128]{2,1,0:T(8,128)(2,1)S(1)}, u32[]{:S(2)}, u32[]{:S(2)}) collective-permute-start(f16[49,8,128]{2,1,0:T(8,128)(2,1)S(1)} %convert_element_type.22), channel_id=1, source_target_pairs={{0,2},{1,31},{2,0},{3,1},{4,6},{5,3},{6,4},{7,5},{8,10},{9,7},{10,... | collective-permute-start | bytes 301064 | tf_op jit(solution)/shard_map/ppermute | solution.py:194
